TPU v7x, 32 devices: a whole 2x2x4 slice. The times are simulated.
32 devices in a mesh: pairs: 8 (over y, x, core), coef: 4 (over z).
Axes of the slice: x: 2, y: 2, z: 4, core: 2. Of those that a mesh axis runs over, the one named last changes fastest.
Arguments:
- integrals: bfloat16 [4096, 32, 64, 64], P('pairs', 'coef'), may hold values from -6 to 6
- block_shells: int32 [8, 32, 2], P('pairs', 'coef'), may hold values from 0 to 143
- live_counts: int32 [8, 4], P('pairs', 'coef'), may hold values from 1 to 8, as said below
- significance: int32 [144, 144], replicated, may hold values 0 or 1
- occ_coef: bfloat16 [9216, 64], P('coef'), may hold values from -0.375 to 0.375
- lam_coef: bfloat16 [64, 128], P('coef'), may hold values from -0.75 to 0.75
- sig_coef: bfloat16 [64, 128], P('coef'), may hold values from -0.75 to 0.75
Outputs:
- mo_integrals: float32 [4096, 128, 128], P(('pairs', 'coef'))
Inputs may be any that keep to these rules, and one draw needn't show every extreme that they name: `live_counts`: each device's live slots are its first ones; some device has all 8 live.
All inputs are finite; a program needn't handle non-finite values.
Results may differ from a plain program's by a relative error of at most 0.0029.
Values may be sent and summed in bfloat16 or wider, within the bound.
A program may use at most 128 MiB of HBM per device.

v0:
```python
import jax
import jax.numpy as jnp
from jax import lax
from jax.sharding import PartitionSpec as P


def on_device(integrals, block_shells, live_counts, significance, occ_coef, lam_coef, sig_coef):
    occupied, lam_panel, sig_panel = (
        lax.all_gather(occ_coef, "coef", axis=0, tiled=True),
        lax.all_gather(lam_coef, "coef", axis=0, tiled=True),
        lax.all_gather(sig_coef, "coef", axis=0, tiled=True),
    )
    shell_size = integrals.shape[2]
    slot_count = integrals.shape[1]
    local_pairs = integrals.shape[0]
    occ_count = occupied.shape[1]
    shell_table = occupied.reshape(-1, shell_size, occ_count)
    pair_shells = block_shells[0]
    row_shells = shell_table[pair_shells[:, 0]]
    col_shells = shell_table[pair_shells[:, 1]]
    screened = significance[pair_shells[:, 0], pair_shells[:, 1]]
    live_total = live_counts[0, 0]
    is_live = (jnp.arange(slot_count) < live_total) & (screened == 1)
    col_weighted = col_shells * is_live.astype(jnp.bfloat16)[:, None, None]
    quarter = jnp.einsum(
        "smi,lsmn->lsin", row_shells, integrals, preferred_element_type=jnp.float32
    ).astype(jnp.bfloat16)
    partial_sums = jnp.einsum(
        "lsin,snj->ijl", quarter, col_weighted, preferred_element_type=jnp.float32
    )
    flat_sums = partial_sums.reshape(occ_count * occ_count, local_pairs)
    moved = lax.all_to_all(flat_sums, "pairs", split_axis=0, concat_axis=1, tiled=True)
    owned = lax.psum_scatter(moved, "coef", scatter_dimension=0, tiled=True)
    lam_width = lam_panel.shape[0]
    sig_width = sig_panel.shape[0]
    owned_grid = owned.reshape(owned.shape[0], lam_width, sig_width)
    partly = jnp.einsum(
        "xa,qxy->qay", lam_panel.astype(jnp.float32), owned_grid, precision=lax.Precision.HIGHEST
    )
    return jnp.einsum(
        "qay,yb->qab", partly, sig_panel.astype(jnp.float32), precision=lax.Precision.HIGHEST
    )


def solution(mesh):
    placed = (
        P("pairs", "coef", None, None),
        P("pairs", "coef", None),
        P("pairs", "coef"),
        P(),
        P("coef", None),
        P("coef", None),
        P("coef", None),
    )
    return jax.shard_map(
        on_device,
        mesh=mesh,
        in_specs=placed,
        out_specs=P(("pairs", "coef"), None, None),
        check_vma=False,
    )
```

profile of v0, /device:TPU:0, one launch (start us, length us, event | category | flops | bytes accessed | tf_op | source)
XLA Modules:
  0.0 459.4 jit_solution(7912508997936491548)
XLA Ops:
  6.5 0.0 copy-start
  6.5 0.0 all-gather.2.cloned.1.call-start
  6.5 0.7 all-gather.2.cloned.1.call-update
  7.3 0.0 reduce-scatter.2.cloned.1.call-start
  8.0 0.8 or_bitcast_fusion
  8.7 0.0 copy-done
  8.7 0.6 gather_fusion.1
  9.4 32.7 %all-gather.2.cloned.1.call-done = bf16[9216,64]{0,1:T(8,128)(2,1)} async-done(((bf16[2304,64]{0,1:T(8,128)(2,1)}), bf16[9216,64]{0,1:T(8,128)(2,1)}) %all-gather.2.cloned.1.call-update) | async-done | bytes 1179664 | tf_op jit(solution)/shard_map/all_gather | solution.py:9
  42.1 2.8 copy.19
  44.9 0.6 gather_fusion.2
  45.5 0.6 gather_fusion
  46.0 58.2 %fusion.3 = bf16[8,64,512,64]{2,1,3,0:T(8,128)(2,1)} fusion(bf16[512,8,64,64]{0,3,2,1:T(8,128)(2,1)} %param.7, bf16[8,64,64]{2,1,0:T(8,128)(2,1)S(1)} %gather_fusion.2), kind=kOutput, calls=%fused_computation.6 | convolution fusion | flops 2147483648 | bytes 67174400 | tf_op jit(solution)/shard_map/smi,lsmn->lsin/dot_general | solution.py:25
  104.3 77.8 %fusion.1 = f32[64,512,64,1]{1,0,3,2:T(8,128)} fusion(bf16[8,64,512,64]{2,1,3,0:T(8,128)(2,1)} %fusion.3, bf16[8,64,64]{2,1,0:T(8,128)(2,1)S(1)} %gather_fusion, bf16[8]{0:T(256)(128)(2,1)S(1)} %and_convert_fusion), kind=kOutput, calls=%fused_computation.5 | convolution fusion | flops 2147614720 | bytes 42008592 | tf_op jit(solution)/shard_map/lsin,snj->ijl/dot_general | solution.py:28
  182.1 9.1 %copy.11 = f32[8,512,512]{1,2,0:T(8,128)} copy(f32[8,512,512]{2,1,0:T(8,128)} %bitcast.42) | data formatting | bytes 16777216 | tf_op jit(solution)/shard_map/all_to_all | solution.py:32
  191.2 99.7 %all_to_all.19 = f32[8,512,512]{1,2,0:T(8,128)} all-to-all(f32[8,512,512]{1,2,0:T(8,128)} %copy.11), channel_id=1, replica_groups=mesh['pairs'=8,'coef'=4] {'pairs'}, dimensions={0} | all-to-all | bytes 16777216 | tf_op jit(solution)/shard_map/all_to_all | solution.py:32
  290.9 0.0 copy-start.2
  290.9 0.0 copy-start.3
  290.9 0.0 reduce-scatter.2.cloned.1.call-update
  291.0 0.7 copy-done.2
  291.6 13.4 %all_gather.10 = bf16[64,128]{1,0:T(8,128)(2,1)S(1)} all-gather(bf16[16,128]{1,0:T(8,128)(2,1)S(1)} %copy-done.2), channel_id=1, replica_groups=mesh['pairs'=8,'coef'=4] {'coef'}, dimensions={0}, use_global_device_ids=true | all-gather | bytes 20480 | tf_op jit(solution)/shard_map/all_gather | solution.py:10
  305.0 0.0 copy-done.3
  305.0 13.4 %all_gather.11 = bf16[64,128]{1,0:T(8,128)(2,1)S(1)} all-gather(bf16[16,128]{1,0:T(8,128)(2,1)S(1)} %copy-done.3), channel_id=1, replica_groups=mesh['pairs'=8,'coef'=4] {'coef'}, dimensions={0}, use_global_device_ids=true | all-gather | bytes 20480 | tf_op jit(solution)/shard_map/all_gather | solution.py:11
  318.4 114.9 %reduce-scatter.2.cloned.1.call-done = f32[128,4096]{0,1:T(8,128)} async-done(((f32[512,4096]{0,1:T(8,128)}), f32[128,4096]{0,1:T(8,128)}) %reduce-scatter.2.cloned.1.call-update) | async-done | bytes 2097168 | tf_op jit(solution)/shard_map/reduce_scatter | solution.py:33
  433.3 5.6 %copy.17 = f32[128,64,64]{1,2,0:T(8,128)} copy(f32[128,64,64]{0,2,1:T(8,128)} %bitcast.45) | data formatting | bytes 4194304 | tf_op jit(solution)/shard_map/reshape | solution.py:36
  438.8 0.0 copy-start.1
  438.8 4.4 fusion.12
  443.2 9.0 %fusion.5 = f32[128,128,128]{2,1,0:T(8,128)} fusion(f32[128,64,128]{2,1,0:T(8,128)S(1)} %fusion.12, bf16[64,128]{1,0:T(8,128)(2,1)S(1)} %all_gather.11), kind=kOutput, calls=%fused_computation.8 | convolution fusion | flops 1610612736 | bytes 12599296 | tf_op jit(solution)/shard_map/qay,yb->qab/dot_general | solution.py:40
  452.2 0.0 copy-done.1
  (2 shorter events, 0.0 us)
Async XLA Ops:
  6.5 2.2 copy-start
  6.5 35.6 %all-gather.2.cloned.1.call-start = ((), (), s32[]{:S(2)}) async-start(), calls=%async_computation.2 | async-start | bytes 1474560 | tf_op jit(solution)/shard_map/all_gather | solution.py:9
  7.3 426.0 %reduce-scatter.2.cloned.1.call-start = ((), (), s32[]{:S(2)}) async-start(), calls=%async_computation.3 | async-start | bytes 10485760 | tf_op jit(solution)/shard_map/reduce_scatter | solution.py:33
  290.9 0.7 copy-start.2
  290.9 14.1 %copy-start.3 = (bf16[16,128]{1,0:T(8,128)(2,1)S(1)}, bf16[16,128]{1,0:T(8,128)(2,1)}, u32[]{:S(2)}) copy-start(bf16[16,128]{1,0:T(8,128)(2,1)} %param.13) | copy-start | bytes 12292
  438.8 13.4 %copy-start.1 = (s32[144,144]{1,0:T(8,128)S(1)}, s32[144,144]{1,0:T(8,128)}, u32[]{:S(2)}) copy-start(s32[144,144]{1,0:T(8,128)} %param.10) | copy-start | bytes 248836
Sparse Core Ops, SparseCore 0:
  8.9 33.1 all-gather.1
  291.1 142.1 reduce-scatter.1
where the time goes:
time: 469 us; the launch traced here: 459 us
  matrix products  149 us (32%)
  waiting for transfers between devices  148 us (32%)
  blocking collectives  126 us (27%)
  local copies, waits for them, and re-layouts  19.9 us (4%)
  between operations  14.5 us (3%)
    reduce_scatter x1, waiting for transfers between devices, on_device(): owned = lax.psum_scatter(moved, 'coef', scatter_dimension=0, tiled=True)  115 us
    all_to_all x1, blocking collectives, on_device(): lax.all_to_all(flat_sums, 'pairs', split_axis=0, concat_axis=1, tiled=True)  99.7 us
    dot_general x1, matrix products, on_device(): jnp.einsum('lsin,snj->ijl', quarter, col_weighted, preferred_element_type...  77.8 us
    dot_general x1, matrix products, on_device(): jnp.einsum('smi,lsmn->lsin', row_shells, integrals, preferred_element_typ...  58.2 us
    all_gather x1, waiting for transfers between devices, on_device(): lax.all_gather(occ_coef, 'coef', axis=0, tiled=True)  32.7 us
    all_gather x1, blocking collectives, on_device(): lax.all_gather(lam_coef, 'coef', axis=0, tiled=True)  13.4 us
    all_gather x1, blocking collectives, on_device(): lax.all_gather(sig_coef, 'coef', axis=0, tiled=True)  13.4 us
  transfers between devices with their start and end apart: 2, of which 2 were waited for; matrix products, arithmetic and copies ran while one was open for 0% of the time, Pallas kernels for 0%

commit v1 on v0

v1 whole, which is shorter than its diff:
```python
import functools

import jax
import jax.numpy as jnp
from jax import lax
from jax.experimental import pallas as pl
from jax.experimental.pallas import tpu as pltpu
from jax.sharding import PartitionSpec as P

LANES = 256
SUB = 4


def spread(block, inner, outer, first, second):
    a, b = block.shape
    rows = lax.broadcasted_iota(jnp.int32, (outer, a), 0)
    cols = lax.broadcasted_iota(jnp.int32, (outer, a), 1)
    pick_a = (first(rows) == cols).astype(jnp.bfloat16)
    rows = lax.broadcasted_iota(jnp.int32, (b, inner), 0)
    cols = lax.broadcasted_iota(jnp.int32, (b, inner), 1)
    pick_b = (second(cols) == rows).astype(jnp.bfloat16)
    left = jnp.dot(pick_a, block, preferred_element_type=jnp.float32).astype(jnp.bfloat16)
    return jnp.dot(left, pick_b, preferred_element_type=jnp.float32)


def half_kernel(row_ref, col_ref, tiles_ref, out_ref, lhs1, lhs2, wide, quarter):
    tile, slot = pl.program_id(0), pl.program_id(1)
    slots = pl.num_programs(1)
    shell = tiles_ref.shape[1]
    occ = row_ref.shape[1]
    k1 = SUB * shell
    n1 = SUB * occ
    k2 = SUB * shell
    n2 = SUB * occ

    @pl.when(tile == 0)
    def _():
        body = spread(row_ref[0], k1, n1, lambda r: r // SUB, lambda c: c % shell)
        r = lax.broadcasted_iota(jnp.int32, (n1, k1), 0)
        c = lax.broadcasted_iota(jnp.int32, (n1, k1), 1)
        lhs1[slot] = jnp.where(r % SUB == c // shell, body, 0.0).astype(jnp.bfloat16)
        body = spread(
            col_ref[0], k2, n2, lambda r: r % occ,
            lambda c: c // (SUB * SUB) * SUB + c % SUB,
        )
        r = lax.broadcasted_iota(jnp.int32, (n2, k2), 0)
        c = lax.broadcasted_iota(jnp.int32, (n2, k2), 1)
        lhs2[slot] = jnp.where(r // occ == c // SUB % SUB, body, 0.0).astype(jnp.bfloat16)

    wide[...] = tiles_ref[0].astype(jnp.float32)
    coef = lhs1[slot]
    step = SUB * SUB
    for q in range(shell // SUB):
        packed = jnp.concatenate(
            [wide[:, q * SUB + n, :].astype(jnp.bfloat16) for n in range(SUB)], axis=0
        )
        got = jnp.dot(coef, packed, preferred_element_type=jnp.float32).astype(jnp.bfloat16)
        quarter[slot, :, q * step:(q + 1) * step, :] = got.reshape(occ // SUB, step, got.shape[1])

    @pl.when(slot == slots - 1)
    def _():
        def one(iq, _):
            total = jnp.zeros((n2, out_ref.shape[1]), jnp.float32)
            for s in range(quarter.shape[0]):
                total = total + jnp.dot(lhs2[s], quarter[s, iq], preferred_element_type=jnp.float32)
            out_ref[pl.ds(pl.multiple_of(iq * n2, n2), n2), :] = total.astype(out_ref.dtype)
            return 0

        lax.fori_loop(0, occ // SUB, one, 0)


def half_sums(row_t, col_t, tiles):
    slots, shell, _, pairs = tiles.shape
    occ = row_t.shape[1]
    lanes = min(LANES, pairs)
    k = SUB * shell
    return pl.pallas_call(
        half_kernel,
        grid=(pairs // lanes, slots),
        out_shape=jax.ShapeDtypeStruct((occ * occ, pairs), jnp.bfloat16),
        in_specs=[
            pl.BlockSpec((1, occ, shell), lambda t, s: (s, 0, 0)),
            pl.BlockSpec((1, occ, shell), lambda t, s: (s, 0, 0)),
            pl.BlockSpec((1, shell, shell, lanes), lambda t, s: (s, 0, 0, t)),
        ],
        out_specs=pl.BlockSpec((occ * occ, lanes), lambda t, s: (0, t)),
        scratch_shapes=[
            pltpu.VMEM((slots, SUB * occ, k), jnp.bfloat16),
            pltpu.VMEM((slots, SUB * occ, k), jnp.bfloat16),
            pltpu.VMEM((shell, shell, lanes), jnp.float32),
            pltpu.VMEM((slots, occ // SUB, k, lanes), jnp.bfloat16),
        ],
        compiler_params=pltpu.CompilerParams(vmem_limit_bytes=48 * 2**20),
        name="half_sums",
    )(row_t, col_t, tiles)


def on_device(integrals, block_shells, live_counts, significance, occ_coef, lam_coef, sig_coef):
    occupied = lax.all_gather(occ_coef, "coef", axis=0, tiled=True)
    lam_panel = lax.all_gather(lam_coef, "coef", axis=0, tiled=True)
    sig_panel = lax.all_gather(sig_coef, "coef", axis=0, tiled=True)
    shell = integrals.shape[2]
    slots = integrals.shape[1]
    pairs = integrals.shape[0]
    occ = occupied.shape[1]
    table = occupied.reshape(-1, shell, occ)
    pair_shells = block_shells[0]
    rows = table[pair_shells[:, 0]]
    cols = table[pair_shells[:, 1]]
    screened = significance[pair_shells[:, 0], pair_shells[:, 1]]
    is_live = (jnp.arange(slots) < live_counts[0, 0]) & (screened == 1)
    cols = cols * is_live.astype(jnp.bfloat16)[:, None, None]
    half = half_sums(
        jnp.swapaxes(rows, 1, 2), jnp.swapaxes(cols, 1, 2), jnp.transpose(integrals, (1, 2, 3, 0))
    )
    n_pairs, n_coef = lax.axis_size("pairs"), lax.axis_size("coef")
    owners = n_pairs * n_coef
    owned_rows = occ * occ // owners
    moved = lax.all_to_all(
        half.reshape(owners, owned_rows, pairs), ("pairs", "coef"), split_axis=0, concat_axis=0, tiled=True
    )
    moved = moved.reshape(n_pairs, n_coef, owned_rows, pairs).astype(jnp.float32)
    owned = jnp.sum(moved, axis=1)
    lam_width, sig_width = lam_panel.shape[0], sig_panel.shape[0]
    grid = jnp.transpose(owned, (1, 0, 2)).reshape(owned_rows, lam_width, sig_width)
    partly = jnp.einsum(
        "xa,qxy->qay", lam_panel.astype(jnp.float32), grid, precision=lax.Precision.HIGHEST
    )
    return jnp.einsum(
        "qay,yb->qab", partly, sig_panel.astype(jnp.float32), precision=lax.Precision.HIGHEST
    )


def solution(mesh):
    placed = (
        P("pairs", "coef", None, None),
        P("pairs", "coef", None),
        P("pairs", "coef"),
        P(),
        P("coef", None),
        P("coef", None),
        P("coef", None),
    )
    return jax.shard_map(
        on_device,
        mesh=mesh,
        in_specs=placed,
        out_specs=P(("pairs", "coef"), None, None),
        check_vma=False,
    )
```

time: 469 us -> 292 us (0.62); the launches traced: 459 us -> 292 us
  matrix products: 149 us -> 13.4 us
  waiting for transfers between devices: 148 us -> 33.5 us
  Pallas kernels: 0 us -> 95.7 us
  blocking collectives: 126 us -> 113 us
  local copies, waits for them, and re-layouts: 19.9 us -> 14.3 us
    dot_general x3 -> x1, matrix products: 140 us -> 4.39 us  [on_device(): jnp.einsum('xa,qxy->qay', lam_panel.astype(jnp.float32), grid, precision=...]
    reduce_scatter x1 -> x0, waiting for transfers between devices: 115 us -> none  [on_device(): owned = lax.psum_scatter(moved, 'coef', scatter_dimension=0, tiled=True)]
    all_to_all x1 -> x0, blocking collectives: 99.7 us -> none  [on_device(): lax.all_to_all(flat_sums, 'pairs', split_axis=0, concat_axis=1, tiled=True)]
    pallas_call x0 -> x1, Pallas kernels: none -> 95.7 us  [half_sums(): pl.pallas_call(half_kernel, grid=(pairs // lanes, slots), out_shape=jax.S...]
    all_gather x2, blocking collectives: 26.8 us -> 113 us  [the longest x1 100 us: on_device(): lam_panel = lax.all_gather(lam_coef, 'coef', axis=0, tiled=True)]
    all_to_all x1 -> x0, local copies, waits for them, and re-layouts: 9.13 us -> none  [on_device(): lax.all_to_all(flat_sums, 'pairs', split_axis=0, concat_axis=1, tiled=True)]
  transfers between devices with their start and end apart: 2 -> 2, of which waited for: 2 -> 1; matrix products, arithmetic and copies ran while one was open for 0% -> 0% of each run, Pallas kernels for 0% -> 0%
where the time goes in v1:
time: 292 us
  blocking collectives  113 us (39%)
  Pallas kernels  95.7 us (33%)
  waiting for transfers between devices  33.5 us (11%)
  local copies, waits for them, and re-layouts  14.3 us (5%)
  between operations  14.1 us (5%)
  matrix products  13.4 us (5%)
  other arithmetic  3.97 us (1%)
  starting transfers between devices  3.8 us (1%)
    all_gather x1, blocking collectives, on_device(): lam_panel = lax.all_gather(lam_coef, 'coef', axis=0, tiled=True)  100 us
    pallas_call x1, Pallas kernels, half_sums(): pl.pallas_call(half_kernel, grid=(pairs // lanes, slots), out_shape=jax.S...  95.7 us
    all_gather x1, waiting for transfers between devices, on_device(): occupied = lax.all_gather(occ_coef, 'coef', axis=0, tiled=True)  32.8 us
    all_gather x1, blocking collectives, on_device(): sig_panel = lax.all_gather(sig_coef, 'coef', axis=0, tiled=True)  13.3 us
    dot_general x1, matrix products, on_device(): jnp.einsum('qay,yb->qab', partly, sig_panel.astype(jnp.float32), precisio...  8.99 us
  transfers between devices with their start and end apart: 2, of which 1 were waited for; matrix products, arithmetic and copies ran while one was open for 0% of the time, Pallas kernels for 0%

profile of v1, /device:TPU:0, one launch (start us, length us, event | category | flops | bytes accessed | tf_op | source)
XLA Modules:
  0.0 292.1 jit_solution(15199983816285763883)
XLA Ops:
  6.5 0.0 copy-start
  6.5 0.0 all-gather.2.cloned.1.call-start
  6.5 0.7 all-gather.2.cloned.1.call-update
  7.9 0.8 or_bitcast_fusion
  8.7 0.0 copy-done
  8.7 0.6 gather_fusion.2
  9.3 32.8 %all-gather.2.cloned.1.call-done = bf16[9216,64]{0,1:T(8,128)(2,1)} async-done(((bf16[2304,64]{0,1:T(8,128)(2,1)}), bf16[9216,64]{0,1:T(8,128)(2,1)}) %all-gather.2.cloned.1.call-update) | async-done | bytes 1179664 | tf_op jit(solution)/shard_map/all_gather | solution.py:99
  42.1 2.8 copy.18
  44.9 0.6 gather_fusion.1
  45.5 0.6 gather_fusion
  46.0 0.1 copy.13
  46.2 0.1 copy.15
  46.3 0.1 multiply_bitcast_fusion.col_ref
  46.4 95.7 %half_sums.1 = bf16[4096,512]{1,0:T(8,128)(2,1)S(1)} custom-call(bf16[8,64,64]{2,1,0:T(8,128)(2,1)S(1)} %bitcast.31, bf16[8,64,64]{2,1,0:T(8,128)(2,1)S(1)} %multiply_bitcast_fusion.col_ref, bf16[8,64,64,512]{3,2,1,0:T(8,128)(2,1)} %bitcast.32), custom_call_target="tpu_custom_call" | custom-call | tf_op jit(solution)/shard_map/half_sums/pallas_call | solution.py:77
  142.1 0.0 copy-start.2
  142.1 2.0 copy-done.2
  144.1 0.0 copy-start.3
  144.1 0.0 copy-start.4
  144.1 3.8 %all-to-all-start = ((bf16[32,128,512]{2,1,0:T(8,128)(2,1)}), bf16[32,128,512]{2,1,0:T(8,128)(2,1)}, u32[]{:S(2)}, u32[]{:S(2)}) async-start(bf16[32,128,512]{2,1,0:T(8,128)(2,1)} %bitcast.30), calls=%async_computation | async-start | bytes 8388608 | tf_op jit(solution)/shard_map/all_to_all | solution.py:119
  147.9 0.0 copy-done.3
  147.9 100.1 %all_gather.10 = bf16[64,128]{1,0:T(8,128)(2,1)S(1)} all-gather(bf16[16,128]{1,0:T(8,128)(2,1)S(1)} %copy-done.3), channel_id=1, replica_groups=mesh['pairs'=8,'coef'=4] {'coef'}, dimensions={0}, use_global_device_ids=true | all-gather | bytes 20480 | tf_op jit(solution)/shard_map/all_gather | solution.py:100
  248.0 0.0 copy-done.4
  248.0 13.3 %all_gather.11 = bf16[64,128]{1,0:T(8,128)(2,1)S(1)} all-gather(bf16[16,128]{1,0:T(8,128)(2,1)S(1)} %copy-done.4), channel_id=1, replica_groups=mesh['pairs'=8,'coef'=4] {'coef'}, dimensions={0}, use_global_device_ids=true | all-gather | bytes 20480 | tf_op jit(solution)/shard_map/all_gather | solution.py:101
  261.3 0.0 all-to-all-done
  261.3 3.1 %convert_reduce_fusion = f32[8,128,512]{2,1,0:T(8,128)S(1)} fusion(bf16[32,128,512]{2,1,0:T(8,128)(2,1)} %all-to-all-done), kind=kLoop, calls=%fused_computation.3 | loop fusion | flops 3670016 | bytes 6291456 | tf_op jit(solution)/shard_map/reduce_sum | solution.py:123
  264.4 1.9 copy.16
  266.3 5.6 %copy.17 = f32[128,64,64]{1,2,0:T(8,128)} copy(f32[128,64,64]{0,2,1:T(8,128)} %bitcast.34) | data formatting | bytes 4194304 | tf_op jit(solution)/shard_map/reshape | solution.py:125
  271.9 0.0 copy-start.1
  271.9 4.4 %fusion.3 = f32[128,64,128]{2,1,0:T(8,128)S(1)} fusion(f32[128,64,64]{1,2,0:T(8,128)} %copy.17, bf16[64,128]{1,0:T(8,128)(2,1)S(1)} %all_gather.10), kind=kOutput, calls=%fused_computation.8 | convolution fusion | flops 805306368 | bytes 6307840 | tf_op jit(solution)/shard_map/xa,qxy->qay/dot_general | solution.py:126
  276.3 9.0 %fusion = f32[128,128,128]{2,1,0:T(8,128)} fusion(f32[128,64,128]{2,1,0:T(8,128)S(1)} %fusion.3, bf16[64,128]{1,0:T(8,128)(2,1)S(1)} %all_gather.11), kind=kOutput, calls=%fused_computation.4 | convolution fusion | flops 1610612736 | bytes 12599296 | tf_op jit(solution)/shard_map/qay,yb->qab/dot_general | solution.py:129
  285.3 0.0 copy-done.1
  (2 shorter events, 0.0 us)
Async XLA Ops:
  6.5 2.1 copy-start
  6.5 35.6 %all-gather.2.cloned.1.call-start = ((), (), s32[]{:S(2)}) async-start(), calls=%async_computation.1 | async-start | bytes 1474560 | tf_op jit(solution)/shard_map/all_gather | solution.py:99
  142.1 2.0 copy-start.2
  144.1 3.8 %copy-start.3 = (bf16[16,128]{1,0:T(8,128)(2,1)S(1)}, bf16[16,128]{1,0:T(8,128)(2,1)}, u32[]{:S(2)}) copy-start(bf16[16,128]{1,0:T(8,128)(2,1)} %param.12) | copy-start | bytes 12292
  144.1 103.9 %copy-start.4 = (bf16[16,128]{1,0:T(8,128)(2,1)S(1)}, bf16[16,128]{1,0:T(8,128)(2,1)}, u32[]{:S(2)}) copy-start(bf16[16,128]{1,0:T(8,128)(2,1)} %param.13) | copy-start | bytes 12292
  144.1 117.2 %all-to-all-start = ((bf16[32,128,512]{2,1,0:T(8,128)(2,1)}), bf16[32,128,512]{2,1,0:T(8,128)(2,1)}, u32[]{:S(2)}, u32[]{:S(2)}) async-start(bf16[32,128,512]{2,1,0:T(8,128)(2,1)} %bitcast.30), calls=%async_computation | async-start | bytes 8388608 | tf_op jit(solution)/shard_map/all_to_all | solution.py:119
  271.9 13.4 %copy-start.1 = (s32[144,144]{1,0:T(8,128)S(1)}, s32[144,144]{1,0:T(8,128)}, u32[]{:S(2)}) copy-start(s32[144,144]{1,0:T(8,128)} %param.10) | copy-start | bytes 248836
Sparse Core Ops, SparseCore 0:
  8.9 33.1 all-gather.1

commit v2 on v1

v2 whole, which is shorter than its diff:
```python
import functools

import jax
import jax.numpy as jnp
from jax import lax
from jax.experimental import pallas as pl
from jax.experimental.pallas import tpu as pltpu
from jax.sharding import PartitionSpec as P

LANES = 256
SUB = 4


def spread(block, inner, outer, first, second):
    a, b = block.shape
    rows = lax.broadcasted_iota(jnp.int32, (outer, a), 0)
    cols = lax.broadcasted_iota(jnp.int32, (outer, a), 1)
    pick_a = (first(rows) == cols).astype(jnp.bfloat16)
    rows = lax.broadcasted_iota(jnp.int32, (b, inner), 0)
    cols = lax.broadcasted_iota(jnp.int32, (b, inner), 1)
    pick_b = (second(cols) == rows).astype(jnp.bfloat16)
    left = jnp.dot(pick_a, block, preferred_element_type=jnp.float32).astype(jnp.bfloat16)
    return jnp.dot(left, pick_b, preferred_element_type=jnp.float32)


def half_kernel(row_ref, col_ref, tiles_ref, out_ref, lhs2, wide, quarter):
    slot = pl.program_id(0)
    slots = pl.num_programs(0)
    shell = tiles_ref.shape[1]
    occ = row_ref.shape[1]
    k1 = SUB * shell
    n1 = SUB * occ
    k2 = SUB * shell
    n2 = SUB * occ

    body = spread(row_ref[0], k1, n1, lambda r: r // SUB, lambda c: c % shell)
    r = lax.broadcasted_iota(jnp.int32, (n1, k1), 0)
    c = lax.broadcasted_iota(jnp.int32, (n1, k1), 1)
    coef = jnp.where(r % SUB == c // shell, body, 0.0).astype(jnp.bfloat16)
    body = spread(
        col_ref[0], k2, n2, lambda r: r % occ,
        lambda c: c // (SUB * SUB) * SUB + c % SUB,
    )
    r = lax.broadcasted_iota(jnp.int32, (n2, k2), 0)
    c = lax.broadcasted_iota(jnp.int32, (n2, k2), 1)
    lhs2[slot] = jnp.where(r // occ == c // SUB % SUB, body, 0.0).astype(jnp.bfloat16)

    lanes = tiles_ref.shape[3]
    for h in range(lanes // 128):
        part = tiles_ref[0, :, :, h * 128:(h + 1) * 128].astype(jnp.float32)
        wide[h] = part.reshape(shell * shell, 128)
    step = SUB * SUB
    for q in range(shell // SUB):
        packed = jnp.concatenate(
            [
                jnp.concatenate(
                    [
                        wide[h, pl.ds(q * SUB + n, shell, stride=shell), :].astype(jnp.bfloat16)
                        for h in range(lanes // 128)
                    ],
                    axis=1,
                )
                for n in range(SUB)
            ],
            axis=0,
        )
        got = jnp.dot(coef, packed, preferred_element_type=jnp.float32).astype(jnp.bfloat16)
        quarter[slot, :, q * step:(q + 1) * step, :] = got.reshape(occ // SUB, step, got.shape[1])

    @pl.when(slot == slots - 1)
    def _():
        def one(iq, _):
            total = jnp.zeros((n2, out_ref.shape[1]), jnp.float32)
            for s in range(quarter.shape[0]):
                total = total + jnp.dot(lhs2[s], quarter[s, iq], preferred_element_type=jnp.float32)
            out_ref[pl.ds(pl.multiple_of(iq * n2, n2), n2), :] = total.astype(out_ref.dtype)
            return 0

        lax.fori_loop(0, occ // SUB, one, 0)


def half_sums(row_t, col_t, tiles, chunk, lanes):
    slots, shell, _, pairs = tiles.shape
    occ = row_t.shape[1]
    k = SUB * shell
    return pl.pallas_call(
        half_kernel,
        grid=(slots,),
        out_shape=jax.ShapeDtypeStruct((occ * occ, lanes), jnp.bfloat16),
        in_specs=[
            pl.BlockSpec((1, occ, shell), lambda s: (s, 0, 0)),
            pl.BlockSpec((1, occ, shell), lambda s: (s, 0, 0)),
            pl.BlockSpec((1, shell, shell, lanes), lambda s: (s, 0, 0, chunk)),
        ],
        out_specs=pl.BlockSpec((occ * occ, lanes), lambda s: (0, 0)),
        scratch_shapes=[
            pltpu.VMEM((slots, SUB * occ, k), jnp.bfloat16),
            pltpu.VMEM((lanes // 128, shell * shell, 128), jnp.float32),
            pltpu.VMEM((slots, occ // SUB, k, lanes), jnp.bfloat16),
        ],
        compiler_params=pltpu.CompilerParams(vmem_limit_bytes=40 * 2**20),
        cost_estimate=pl.CostEstimate(
            flops=2 * slots * shell * lanes * SUB * (shell * occ + occ * occ),
            bytes_accessed=2 * slots * shell * shell * lanes + 2 * occ * occ * lanes,
            transcendentals=0,
        ),
        name="half_sums",
    )(row_t, col_t, tiles)


def parts_of(x):
    high = x.astype(jnp.bfloat16)
    rest = x - high.astype(jnp.float32)
    mid = rest.astype(jnp.bfloat16)
    return high, mid, (rest - mid.astype(jnp.float32)).astype(jnp.bfloat16)


def virtual_kernel(chunks, *refs):
    moved, (lam_ref, sig_ref, out_ref, turned) = refs[:chunks], refs[chunks:]
    n_pairs, n_coef, rows, lanes = moved[0].shape
    virt = out_ref.shape[2]
    inner = sig_ref.shape[1] // virt
    for k, ref in enumerate(moved):
        total = ref[:, 0].astype(jnp.float32)
        for c in range(1, n_coef):
            total = total + ref[:, c].astype(jnp.float32)
        flat = total.reshape(n_pairs * rows, lanes)
        got = jnp.zeros((n_pairs * rows, inner * virt), jnp.float32)
        for part in reversed(parts_of(flat)):
            got = got + jnp.dot(part, sig_ref[...], preferred_element_type=jnp.float32)
        for x in range(inner):
            turned[k * inner + x] = got[:, x * virt:(x + 1) * virt]
    for q in range(rows):
        body = jnp.concatenate(
            [turned[x, pl.ds(q, n_pairs, stride=rows), :] for x in range(chunks * inner)], axis=0
        )
        out_ref[q] = jnp.dot(
            lam_ref[...], jnp.concatenate(parts_of(body), axis=0), preferred_element_type=jnp.float32
        )


def virtual(moved, lam_panel, sig_panel):
    n_pairs, n_coef, owned_rows, lanes = moved[0].shape
    lam_width, virt = lam_panel.shape
    sig_width = sig_panel.shape[0]
    inner = lanes // sig_width
    outer = len(moved) * inner
    rows = 16
    eye = jnp.eye(inner, dtype=jnp.bfloat16)
    sig_wide = (eye[:, None, :, None] * sig_panel[None, :, None, :]).reshape(lanes, inner * virt)
    lam_turned = lam_panel.reshape(n_pairs, outer, virt).transpose(2, 1, 0).reshape(virt, lam_width)
    lam_wide = jnp.concatenate([lam_turned] * 3, axis=1)
    return pl.pallas_call(
        functools.partial(virtual_kernel, len(moved)),
        grid=(owned_rows // rows,),
        out_shape=jax.ShapeDtypeStruct((owned_rows, virt, virt), jnp.float32),
        in_specs=[pl.BlockSpec((n_pairs, n_coef, rows, lanes), lambda t: (0, 0, t, 0)) for _ in moved]
        + [
            pl.BlockSpec(lam_wide.shape, lambda t: (0, 0)),
            pl.BlockSpec(sig_wide.shape, lambda t: (0, 0)),
        ],
        out_specs=pl.BlockSpec((rows, virt, virt), lambda t: (t, 0, 0)),
        scratch_shapes=[pltpu.VMEM((outer, n_pairs * rows, virt), jnp.float32)],
        compiler_params=pltpu.CompilerParams(vmem_limit_bytes=32 * 2**20),
        name="virtual",
    )(*moved, lam_wide, sig_wide)


def on_device(integrals, block_shells, live_counts, significance, occ_coef, lam_coef, sig_coef):
    occupied = lax.all_gather(occ_coef, "coef", axis=0, tiled=True)
    virt = lam_coef.shape[1]
    both = jnp.concatenate([lam_coef, sig_coef], axis=1)
    both = lax.all_gather(both, "coef", axis=0, tiled=True)
    occupied, both = lax.optimization_barrier((occupied, both))
    lam_panel, sig_panel = both[:, :virt], both[:, virt:]
    shell = integrals.shape[2]
    slots = integrals.shape[1]
    pairs = integrals.shape[0]
    occ = occupied.shape[1]
    table = occupied.reshape(-1, shell, occ)
    pair_shells = block_shells[0]
    rows = table[pair_shells[:, 0]]
    cols = table[pair_shells[:, 1]]
    screened = significance[pair_shells[:, 0], pair_shells[:, 1]]
    is_live = (jnp.arange(slots) < live_counts[0, 0]) & (screened == 1)
    cols = cols * is_live.astype(jnp.bfloat16)[:, None, None]
    row_t, col_t = jnp.swapaxes(rows, 1, 2), jnp.swapaxes(cols, 1, 2)
    tiles = jnp.transpose(integrals, (1, 2, 3, 0))
    n_pairs, n_coef = lax.axis_size("pairs"), lax.axis_size("coef")
    owners = n_pairs * n_coef
    owned_rows = occ * occ // owners
    lanes = min(LANES, pairs)
    sums = []
    for chunk in range(pairs // lanes):
        half = half_sums(row_t, col_t, tiles, chunk, lanes)
        moved = lax.all_to_all(
            half.reshape(owners, owned_rows, lanes), ("pairs", "coef"), split_axis=0, concat_axis=0, tiled=True
        )
        sums.append(moved.reshape(n_pairs, n_coef, owned_rows, lanes))
    return virtual(sums, lam_panel, sig_panel)


def solution(mesh):
    placed = (
        P("pairs", "coef", None, None),
        P("pairs", "coef", None),
        P("pairs", "coef"),
        P(),
        P("coef", None),
        P("coef", None),
        P("coef", None),
    )
    return jax.shard_map(
        on_device,
        mesh=mesh,
        in_specs=placed,
        out_specs=P(("pairs", "coef"), None, None),
        check_vma=False,
    )
```

time: 292 us -> 204 us (0.70)
  blocking collectives: 113 us -> 14.8 us
  waiting for transfers between devices: 33.5 us -> 75.2 us
  Pallas kernels: 95.7 us -> 81.3 us
  matrix products: 13.4 us -> 0 us
  local copies, waits for them, and re-layouts: 14.3 us -> 7.62 us
  starting transfers between devices: 3.8 us -> 8.01 us
    all_gather x2 -> x1, blocking collectives: 113 us -> 14.8 us  [on_device(): both = lax.all_gather(both, 'coef', axis=0, tiled=True)]
    all_to_all x1 -> x2, waiting for transfers between devices: 0.01 us -> 57.2 us  [on_device(): lax.all_to_all(half.reshape(owners, owned_rows, lanes), ('pairs', 'coef')...]
    all_gather x1, waiting for transfers between devices: 32.8 us -> 17.3 us  [on_device(): occupied = lax.all_gather(occ_coef, 'coef', axis=0, tiled=True)]
    pallas_call x1 -> x3, Pallas kernels: 95.7 us -> 81.3 us  [the longest x2 71.6 us: half_sums(): pl.pallas_call(half_kernel, grid=(slots,), out_shape=jax.ShapeDtypeStruct...]
    dot_general x2 -> x0, matrix products: 13.4 us -> none  [the longest x1 8.99 us: on_device(): jnp.einsum('qay,yb->qab', partly, sig_panel.astype(jnp.float32), precisio...]
    reshape x1, local copies, waits for them, and re-layouts: 5.58 us -> 0.11 us  [virtual(): lam_panel.reshape(n_pairs, outer, virt).transpose(2, 1, 0)]
    all_to_all x1 -> x2, starting transfers between devices: 3.8 us -> 8.01 us  [on_device(): lax.all_to_all(half.reshape(owners, owned_rows, lanes), ('pairs', 'coef')...]
    reduce_sum x1 -> x0, other arithmetic: 3.12 us -> none  [on_device(): owned = jnp.sum(moved, axis=1)]
  transfers between devices with their start and end apart: 2 -> 3, of which waited for: 1 -> 3; matrix products, arithmetic and copies ran while one was open for 0% -> 1% of each run, Pallas kernels for 0% -> 18%
where the time goes in v2:
time: 204 us; the launch traced here: 203 us
  Pallas kernels  81.3 us (40%)
  waiting for transfers between devices  75.2 us (37%)
  blocking collectives  14.8 us (7%)
  between operations  14.2 us (7%)
  starting transfers between devices  8.01 us (4%)
  local copies, waits for them, and re-layouts  7.62 us (4%)
    pallas_call x2, Pallas kernels, half_sums(): pl.pallas_call(half_kernel, grid=(slots,), out_shape=jax.ShapeDtypeStruct...  71.6 us
    all_to_all x2, waiting for transfers between devices, on_device(): lax.all_to_all(half.reshape(owners, owned_rows, lanes), ('pairs', 'coef')...  57.2 us
    all_gather x1, waiting for transfers between devices, on_device(): occupied = lax.all_gather(occ_coef, 'coef', axis=0, tiled=True)  17.3 us
    all_gather x1, blocking collectives, on_device(): both = lax.all_gather(both, 'coef', axis=0, tiled=True)  14.8 us
    pallas_call x1, Pallas kernels, virtual(): pl.pallas_call(functools.partial(virtual_kernel, len(moved)), grid=(owned...  9.69 us
    all_to_all x2, starting transfers between devices, on_device(): lax.all_to_all(half.reshape(owners, owned_rows, lanes), ('pairs', 'coef')...  8.01 us
  transfers between devices with their start and end apart: 3, of which 3 were waited for; matrix products, arithmetic and copies ran while one was open for 1% of the time, Pallas kernels for 18%

profile of v2, /device:TPU:0, one launch (start us, length us, event | category | flops | bytes accessed | tf_op | source)
XLA Modules:
  0.0 203.0 jit_solution(10447299177404511436)
XLA Ops:
  6.5 0.0 copy-start
  6.5 0.0 all-gather.2.cloned.1.call-start
  6.5 0.7 all-gather.2.cloned.1.call-update
  7.9 0.8 or_bitcast_fusion
  8.7 0.0 copy-done
  8.7 0.6 gather_fusion.2
  9.3 0.7 pad_maximum_fusion.1
  10.0 14.8 %all_gather.7 = bf16[64,256]{1,0:T(8,128)(2,1)S(1)} all-gather(bf16[16,256]{1,0:T(8,128)(2,1)S(1)} %pad_maximum_fusion.1), channel_id=1, replica_groups=mesh['pairs'=8,'coef'=4] {'coef'}, dimensions={0}, use_global_device_ids=true | all-gather | bytes 40960 | tf_op jit(solution)/shard_map/all_gather | solution.py:173
  24.9 17.3 %all-gather.2.cloned.1.call-done = bf16[9216,64]{0,1:T(8,128)(2,1)} async-done(((bf16[2304,64]{0,1:T(8,128)(2,1)}), bf16[9216,64]{0,1:T(8,128)(2,1)}) %all-gather.2.cloned.1.call-update) | async-done | bytes 1179664 | tf_op jit(solution)/shard_map/all_gather | solution.py:170
  42.2 2.8 %copy.24 = bf16[9216,64]{1,0:T(8,128)(2,1)S(1)} copy(bf16[9216,64]{0,1:T(8,128)(2,1)} %all-gather.2.cloned.1.call-done) | data formatting | bytes 2359296 | tf_op jit(solution)/shard_map/reshape | solution.py:180
  45.0 0.6 gather_fusion.1
  45.5 0.6 gather_fusion
  46.1 0.1 copy.17
  46.3 0.1 copy.19
  46.4 0.1 multiply_bitcast_fusion.col_ref
  46.5 35.8 %half_sums.3 = bf16[4096,256]{1,0:T(8,128)(2,1)S(1)} custom-call(bf16[8,64,64]{2,1,0:T(8,128)(2,1)S(1)} %bitcast.33, bf16[8,64,64]{2,1,0:T(8,128)(2,1)S(1)} %multiply_bitcast_fusion.col_ref, bf16[8,64,64,512]{3,2,1,0:T(8,128)(2,1)} %bitcast.36), custom_call_target="tpu_custom_call" | custom-call | flops 8589934592 | bytes 18874368 | tf_op jit(solution)/shard_map/half_sums/pallas_call | solution.py:86
  82.3 0.0 copy-start.2
  82.3 1.3 copy-done.2
  83.6 3.7 %all-to-all-start.1 = ((bf16[32,128,256]{2,1,0:T(8,128)(2,1)}), bf16[32,128,256]{2,1,0:T(8,128)(2,1)S(1)}, u32[]{:S(2)}, u32[]{:S(2)}) async-start(bf16[32,128,256]{2,1,0:T(8,128)(2,1)} %bitcast.32), calls=%async_computation.1 | async-start | bytes 4194304 | tf_op jit(solution)/shard_map/all_to_all | solution.py:196
  87.4 35.8 %half_sums.2 = bf16[4096,256]{1,0:T(8,128)(2,1)S(1)} custom-call(bf16[8,64,64]{2,1,0:T(8,128)(2,1)S(1)} %bitcast.34, bf16[8,64,64]{2,1,0:T(8,128)(2,1)S(1)} %multiply_bitcast_fusion.col_ref, bf16[8,64,64,512]{3,2,1,0:T(8,128)(2,1)} %bitcast.37), custom_call_target="tpu_custom_call" | custom-call | flops 8589934592 | bytes 18874368 | tf_op jit(solution)/shard_map/half_sums/pallas_call | solution.py:86
  123.2 0.0 copy-start.1
  123.2 1.3 copy-done.1
  124.5 10.4 %all-to-all-done.1 = bf16[32,128,256]{2,1,0:T(8,128)(2,1)S(1)} async-done(((bf16[32,128,256]{2,1,0:T(8,128)(2,1)}), bf16[32,128,256]{2,1,0:T(8,128)(2,1)S(1)}, u32[]{:S(2)}, u32[]{:S(2)}) %all-to-all-start.1) | async-done | bytes 2097184 | tf_op jit(solution)/shard_map/all_to_all | solution.py:196
  134.9 4.3 %all-to-all-start = ((bf16[32,128,256]{2,1,0:T(8,128)(2,1)}), bf16[32,128,256]{2,1,0:T(8,128)(2,1)}, u32[]{:S(2)}, u32[]{:S(2)}) async-start(bf16[32,128,256]{2,1,0:T(8,128)(2,1)} %bitcast.31), calls=%async_computation | async-start | bytes 4194304 | tf_op jit(solution)/shard_map/all_to_all | solution.py:196
  139.2 0.1 copy.21
  139.3 0.2 broadcast_multiply_fusion
  139.6 0.1 pad_maximum_fusion.refs_2_
  139.7 46.8 %all-to-all-done = bf16[32,128,256]{2,1,0:T(8,128)(2,1)} async-done(((bf16[32,128,256]{2,1,0:T(8,128)(2,1)}), bf16[32,128,256]{2,1,0:T(8,128)(2,1)}, u32[]{:S(2)}, u32[]{:S(2)}) %all-to-all-start) | async-done | bytes 2097184 | tf_op jit(solution)/shard_map/all_to_all | solution.py:196
  186.5 9.7 %virtual.1 = f32[128,128,128]{2,1,0:T(8,128)} custom-call(bf16[8,4,128,256]{3,2,1,0:T(8,128)(2,1)} %bitcast.10.refs_0_, bf16[8,4,128,256]{3,2,1,0:T(8,128)(2,1)S(1)} %bitcast.30, bf16[128,192]{1,0:T(8,128)(2,1)S(1)} %pad_maximum_fusion.refs_2_, bf16[256,512]{1,0:T(8,128)(2,1)S(1)} %bitcast.35), custom_call_target="tpu_custom_call" | custom-call | tf_op jit(solution)/shard_map/virtual/pallas_call | solution.py:153
  (6 shorter events, 0.1 us)
Async XLA Ops:
  6.5 2.1 %copy-start = (s32[144,144]{1,0:T(8,128)S(1)}, s32[144,144]{1,0:T(8,128)}, u32[]{:S(2)}) copy-start(s32[144,144]{1,0:T(8,128)} %param.10) | copy-start | bytes 248836
  6.5 35.7 %all-gather.2.cloned.1.call-start = ((), (), s32[]{:S(2)}) async-start(), calls=%async_computation.2 | async-start | bytes 1474560 | tf_op jit(solution)/shard_map/all_gather | solution.py:170
  82.3 1.3 copy-start.2
  83.6 51.3 %all-to-all-start.1 = ((bf16[32,128,256]{2,1,0:T(8,128)(2,1)}), bf16[32,128,256]{2,1,0:T(8,128)(2,1)S(1)}, u32[]{:S(2)}, u32[]{:S(2)}) async-start(bf16[32,128,256]{2,1,0:T(8,128)(2,1)} %bitcast.32), calls=%async_computation.1 | async-start | bytes 4194304 | tf_op jit(solution)/shard_map/all_to_all | solution.py:196
  123.2 1.3 copy-start.1
  134.9 51.6 %all-to-all-start = ((bf16[32,128,256]{2,1,0:T(8,128)(2,1)}), bf16[32,128,256]{2,1,0:T(8,128)(2,1)}, u32[]{:S(2)}, u32[]{:S(2)}) async-start(bf16[32,128,256]{2,1,0:T(8,128)(2,1)} %bitcast.31), calls=%async_computation | async-start | bytes 4194304 | tf_op jit(solution)/shard_map/all_to_all | solution.py:196
Sparse Core Ops, SparseCore 0:
  8.9 33.2 all-gather.1
